TPU v7x, 512 devices: a whole 4x4x16 slice. The times are simulated.
512 devices in a mesh: gx: 16 (over z), gy: 32 (over x, y, core).
Axes of the slice: x: 4, y: 4, z: 16, core: 2. Of those that a mesh axis runs over, the one named last changes fastest.
Arguments:
- particles: bfloat16 [32768, 4096], P(('gx', 'gy')), may hold values from -6 to 6
- references: bfloat16 [16, 12, 4096], P('gx'), may hold values from -1 to 1
- slot_class: int32 [16], replicated, may hold values from 0 to 15, each once
- log_prior: float32 [16], replicated, may hold values from -2 to 2
- shift_offsets: int32 [8, 2], replicated, may hold values from -8 to 8
- group_ids: int32 [32768], P(('gx', 'gy')), may hold values from 0 to 127
- ctf_table: float32 [128, 2048], replicated, may hold values from -1 to 1
- noise_power: float32 [2048], replicated, may hold values from 0.5 to 2
Outputs:
- class_sums: float32 [16, 12, 4096], P('gx')
- ctf_power: float32 [16, 2048], P('gx')
- log_evidence: float32 [], replicated
Inputs may be any that keep to these rules, and one draw needn't show every extreme that they name: `slot_class`: each class id stands at exactly one slot.
All inputs are finite; a program needn't handle non-finite values.
Results may differ from a plain program's by a relative error of at most 0.006.
Values may be sent and summed in bfloat16 or wider, within the bound.
A program may use at most 64 MiB of HBM per device.

v0:
```python
import functools

import jax
import jax.numpy as jnp
from jax import lax
from jax.sharding import Mesh
from jax.sharding import PartitionSpec as P

L = 64
R = 12
NS = 8
G = 128
HALF = 2048
FR = 4096
GY = ("gy_0", "gy_1", "gy_2")
GX_GY = ("gx", "gy_0", "gy_1", "gy_2")


def in_blocks(shard, dim, length):
    before, after = (shard.shape[:dim], shard.shape[dim + 1 :])
    return jnp.moveaxis(shard.reshape(*before, length, -1, *after), dim, 0)


def summed_on_arrival(shard, axis, dim):
    tiles = in_blocks(shard, dim, lax.axis_size(axis))
    arrived = lax.all_to_all(tiles, axis, split_axis=0, concat_axis=0, tiled=True)
    return arrived.sum(axis=0)


def gathered_total(shard, axis):
    return lax.all_gather(shard, axis).sum(0)


def over_axes(shard, axes):
    return functools.reduce(lax.psum, axes, shard)


def phase_tables(shift_offsets, edge_len):
    half_size = edge_len * edge_len // 2
    freq_index = jnp.arange(half_size, dtype=jnp.int32)
    row_freq = freq_index // (edge_len // 2)
    col_freq = freq_index % (edge_len // 2)
    phase_turns = jnp.mod(
        row_freq[None, :] * shift_offsets[:, 0:1] + col_freq[None, :] * shift_offsets[:, 1:2],
        edge_len,
    )
    angles = phase_turns.astype(jnp.float32) * (2.0 * jnp.pi / edge_len)
    return (jnp.cos(angles), jnp.sin(angles))


def spectra(particles, edge_len):
    rows_here = particles.shape[0]
    half_side = edge_len // 2
    images = particles.astype(jnp.float32).reshape(rows_here * edge_len, edge_len)
    pixel_index = jnp.arange(edge_len, dtype=jnp.int32)
    column_turns = jnp.mod(pixel_index[:, None] * pixel_index[None, :half_side], edge_len).astype(
        jnp.float32
    ) * (2.0 * jnp.pi / edge_len)
    column_table = jnp.concatenate([jnp.cos(column_turns), -jnp.sin(column_turns)], axis=1)
    partial_x = jnp.dot(
        images, column_table, precision=lax.Precision.HIGHEST, preferred_element_type=jnp.float32
    )
    partial_x = partial_x.reshape(rows_here, edge_len, edge_len)
    row_turns = jnp.mod(pixel_index[:, None] * pixel_index[None, :], edge_len).astype(
        jnp.float32
    ) * (2.0 * jnp.pi / edge_len)
    with_cos = jnp.einsum(
        "uy,pyw->puw", jnp.cos(row_turns), partial_x, precision=lax.Precision.HIGHEST
    )
    with_sin = jnp.einsum(
        "uy,pyw->puw", jnp.sin(row_turns), partial_x, precision=lax.Precision.HIGHEST
    )
    real_part = (with_cos[..., :half_side] + with_sin[..., half_side:]) / edge_len
    imag_part = (with_cos[..., half_side:] - with_sin[..., :half_side]) / edge_len
    return (real_part.reshape(rows_here, -1), imag_part.reshape(rows_here, -1))


def shards(
    particles, references, slot_class, log_prior, shift_offsets, group_ids, ctf_table, noise_power
):
    rows_here = particles.shape[0]
    classes = lax.axis_size("gx") * references.shape[0]
    row_width = R * NS
    real_part, imag_part = spectra(particles, L)
    inv_noise = 1.0 / noise_power
    group_hot = (group_ids[:, None] == jnp.arange(G, dtype=jnp.int32)[None, :]).astype(jnp.float32)
    ctf_rows = jnp.dot(
        group_hot, ctf_table, precision=lax.Precision.HIGHEST, preferred_element_type=jnp.float32
    )
    whiten = ctf_rows * inv_noise
    weighted = jnp.concatenate([real_part * whiten, imag_part * whiten], axis=1).astype(
        jnp.bfloat16
    )
    data_power = jnp.sum((real_part * real_part + imag_part * imag_part) * inv_noise, axis=1)
    cosines, sine_table = phase_tables(shift_offsets, L)
    power_table = ctf_table * ctf_table * inv_noise
    blank = jnp.zeros((rows_here, classes * row_width), jnp.float32)
    piece = lax.all_gather(references, "gx", axis=0, tiled=True)

    def add_class(offset, table):
        stack_row = lax.dynamic_index_in_dim(piece, offset, 0, keepdims=False).astype(jnp.float32)
        stack_real = stack_row[:, :HALF]
        stack_imag = stack_row[:, HALF:]
        shifted_real = (
            stack_real[:, None, :] * cosines[None] + stack_imag[:, None, :] * sine_table[None]
        )
        shifted_imag = (
            stack_imag[:, None, :] * cosines[None] - stack_real[:, None, :] * sine_table[None]
        )
        shifted = (
            jnp.concatenate([shifted_real, shifted_imag], axis=2)
            .astype(jnp.bfloat16)
            .reshape(row_width, FR)
        )
        intersection = lax.dot_general(
            weighted, shifted, (((1,), (1,)), ((), ())), preferred_element_type=jnp.float32
        )
        amplitude = stack_real * stack_real + stack_imag * stack_imag
        ref_power = jnp.dot(
            power_table,
            amplitude.T,
            precision=lax.Precision.HIGHEST,
            preferred_element_type=jnp.float32,
        )
        own_power = jnp.dot(
            group_hot,
            ref_power,
            precision=lax.Precision.HIGHEST,
            preferred_element_type=jnp.float32,
        )
        logits = intersection.reshape(rows_here, R, NS) - 0.5 * own_power[:, :, None]
        return lax.dynamic_update_slice_in_dim(
            table, logits.reshape(rows_here, row_width), offset * row_width, 1
        )

    scores = lax.fori_loop(0, piece.shape[0], add_class, blank)
    slot_prior = jnp.sum(
        jnp.where(
            slot_class[:, None] == jnp.arange(classes, dtype=jnp.int32)[None, :],
            log_prior[None, :],
            0.0,
        ),
        axis=1,
    )
    logits = (
        scores.reshape(rows_here, classes, row_width)
        - 0.5 * data_power[:, None, None]
        + slot_prior[None, :, None]
    )
    row_max = jnp.max(logits, axis=(1, 2), keepdims=True)
    raised = jnp.exp(logits - row_max)
    normaliser = jnp.sum(raised, axis=(1, 2), keepdims=True)
    weights = raised / normaliser
    evidence = row_max[:, 0, 0] + jnp.log(normaliser[:, 0, 0])
    weights_low = weights.astype(jnp.bfloat16)
    group_weights = jnp.dot(
        jnp.sum(weights, axis=2).T,
        group_hot,
        precision=lax.Precision.HIGHEST,
        preferred_element_type=jnp.float32,
    )

    def class_terms(slot_index):
        weight_cols = lax.dynamic_index_in_dim(weights_low, slot_index, 1, keepdims=False)
        moment = lax.dot_general(
            weight_cols, weighted, (((0,), (0,)), ((), ())), preferred_element_type=jnp.float32
        )
        moment = moment.reshape(R, NS, FR)
        moment_real = moment[..., :HALF]
        moment_imag = moment[..., HALF:]
        back_real = jnp.sum(moment_real * cosines[None] - moment_imag * sine_table[None], axis=1)
        back_imag = jnp.sum(moment_imag * cosines[None] + moment_real * sine_table[None], axis=1)
        return jnp.concatenate([back_real, back_imag], axis=1)

    owned = summed_on_arrival(
        lax.map(
            lambda offset: class_terms(offset),
            jnp.arange(references.shape[0] * lax.axis_size("gx"), dtype=jnp.int32),
        ),
        "gx",
        0,
    )
    class_sums = gathered_total(owned, GY)
    totals, evidence_sum = (over_axes(group_weights, GX_GY), over_axes(jnp.sum(evidence), GX_GY))
    own_groups = lax.dynamic_slice_in_dim(totals, lax.axis_index("gx"), 1, 0)
    ctf_power = jnp.dot(
        own_groups,
        ctf_table * ctf_table,
        precision=lax.Precision.HIGHEST,
        preferred_element_type=jnp.float32,
    )
    log_evidence = evidence_sum / (rows_here * lax.axis_size("gx") * lax.axis_size(GY) * HALF)
    return (class_sums, ctf_power, log_evidence)


def solution(mesh):
    finer = Mesh(mesh.devices.reshape(mesh.shape["gx"], 4, 4, 2), ("gx", "gy_0", "gy_1", "gy_2"))
    in_specs = (P(GX_GY, None), P("gx", None, None), P(), P(), P(), P(GX_GY), P(), P())
    out_specs = (P("gx", None, None), P("gx", None), P())
    return jax.shard_map(
        shards, mesh=finer, in_specs=in_specs, out_specs=out_specs, check_vma=False
    )
```

profile of v0, /device:TPU:1, one launch (start us, length us, event | category | flops | bytes accessed | tf_op | source)
XLA Modules:
  0.0 449.0 jit_solution(14983572868372554271)
XLA Ops:
  8.1 2.1 reshape.117
  10.2 1.3 convolution_bitcast_fusion.1
  12.5 3.4 fusion.46
  15.9 3.4 fusion.49
  19.9 1.1 copy.47
  21.4 2.0 copy.49
  23.4 1.5 copy.50
  26.2 53.3 %all-gather.5.cloned.1.call-done = bf16[16,12,4096]{2,1,0:T(8,128)(2,1)} async-done(((bf16[1,12,4096]{2,1,0:T(8,128)(2,1)}), bf16[16,12,4096]{2,1,0:T(8,128)(2,1)}) %all-gather.5.cloned.1.call-update) | async-done | bytes 1572880 | tf_op jit(solution)/shard_map/all_gather | solution.py:98
  79.5 60.2 %while.27 = (s32[]{:T(128)}, f32[64,1536]{1,0:T(8,128)S(1)}, bf16[16,12,4096]{2,1,0:T(8,128)(2,1)}, bf16[64,4096]{1,0:T(8,128)(2,1)S(1)}, f32[128,2048]{1,0:T(8,...) while((s32[]{:T(128)}, f32[64,1536]{1,0:T(8,128)S(1)}, ...), condition=%wide.region_1.2_spmd.clone.clone, body=%wide.region_0.1_spmd.clone.clone.sunk | while | flops 92814080 | bytes 4696571 | solution.py:136
  79.6 0.9 bitcast_convert_fusion.2
  83.2 0.9 bitcast_convert_fusion.2
  87.0 0.9 bitcast_convert_fusion.2
  121.0 0.9 bitcast_convert_fusion.2
  140.8 72.5 %while.28 = (s32[]{:T(128)}, f32[16,12,4096]{2,1,0:T(8,128)}, s32[16]{0:T(128)S(1)}, bf16[64,16,96]{0,2,1:T(8,128)(2,1)S(1)}, bf16[64,4096]{1,0:T(8,128)(2,1)S(1...) while((s32[]{:T(128)}, f32[16,12,4096]{2,1,0:T(8,128)}, ...), condition=%wide.region_9.10_spmd.clone.clone, body=%wide.region_6.9_spmd.clone.clone.sunk | while | flops 52166660 | bytes 4629223 | solution.py:176
  213.3 5.5 %copy.54 = f32[16,1,12,4096]{3,1,2,0:T(1,128)S(1)} copy(f32[16,1,12,4096]{3,2,0,1:T(8,128)} %bitcast.10) | data formatting | bytes 6291456 | tf_op jit(solution)/shard_map/reshape | solution.py:21
  218.7 134.6 %all_to_all.5 = f32[16,1,12,4096]{3,1,2,0:T(1,128)S(1)} all-to-all(f32[16,1,12,4096]{3,1,2,0:T(1,128)S(1)} %copy.54), channel_id=1, replica_groups=mesh['gx'=16,'gy_0'=4,'gy_1'=4,'gy_2'=2] {'gx'}, dimensions={0} | all-to-all | bytes 6291456 | tf_op jit(solution)/shard_map/all_to_all | solution.py:26
  353.3 4.3 reduce_sum.86
  358.4 27.7 %all-reduce = (f32[16,128]{1,0:T(8,128)S(1)}, f32[]{:T(128)}) all-reduce(f32[16,128]{1,0:T(8,128)S(1)} %fusion.68, f32[]{:T(128)} %add_reduce_fusion.1), channel_id=1, replica_groups=mesh['gx'=16,'gy_0'=4,'gy_1'=4,'gy_2'=2] {'gx'}, use_global_device_ids=true, to_apply=%region_13.14 | all-reduce | flops 2049 | bytes 16392 | tf_op jit(solution)/shard_map/psum | solution.py:35
  386.1 9.8 %all-reduce.2 = (f32[16,128]{1,0:T(8,128)S(1)}, f32[]{:T(128)}) all-reduce(f32[16,128]{1,0:T(8,128)S(1)} %get-tuple-element.360, f32[]{:T(128)} %get-tuple-element.361), channel_id=1, replica_groups=mesh['gx'=16,'gy_0'=4,'gy_1'=4,'gy_2'=2] {'gy_0'}, use_global_device_ids=true, to_apply=%region_14.15 | all-reduce | flops 2049 | bytes 16392 | tf_op jit(solution)/shard_map/psum | solution.py:35
  395.8 9.3 %all-reduce.1 = (f32[16,128]{1,0:T(8,128)S(1)}, f32[]{:T(128)}) all-reduce(f32[16,128]{1,0:T(8,128)S(1)} %get-tuple-element.364, f32[]{:T(128)} %get-tuple-element.365), channel_id=1, replica_groups=mesh['gx'=16,'gy_0'=4,'gy_1'=4,'gy_2'=2] {'gy_1'}, use_global_device_ids=true, to_apply=%region_15.16 | all-reduce | flops 2049 | bytes 16392 | tf_op jit(solution)/shard_map/psum | solution.py:35
  405.1 25.2 %all-reduce.3 = (f32[16,128]{1,0:T(8,128)S(1)}, f32[]{:T(128)}) all-reduce(f32[16,128]{1,0:T(8,128)S(1)} %get-tuple-element.362, f32[]{:T(128)} %get-tuple-element.363), channel_id=1, replica_groups=mesh['gx'=16,'gy_0'=4,'gy_1'=4,'gy_2'=2] {'gy_2'}, use_global_device_ids=true, to_apply=%region_16.17 | all-reduce | flops 2049 | bytes 16392 | tf_op jit(solution)/shard_map/psum | solution.py:35
  431.0 2.5 fusion.54
  433.4 2.8 all-gather.7.cloned.1.call-done
  436.2 3.9 reduce.5
  (279 shorter events, 103.3 us)
Async XLA Ops:
  7.2 4.3 copy-start.1
  7.2 72.3 %all-gather.5.cloned.1.call-start = ((), (), s32[]{:S(2)}) async-start(), calls=%async_computation.1 | async-start | bytes 2228224 | tf_op jit(solution)/shard_map/all_gather | solution.py:98
  7.9 428.3 %all-gather.7.cloned.1.call-start = ((), (), s32[]{:S(2)}) async-start(), calls=%async_computation.2 | async-start | bytes 8650752 | tf_op jit(solution)/shard_map/all_gather | solution.py:31
  21.3 3.6 copy-start.4
  21.3 3.6 copy-start.5
  21.3 4.0 copy-start.2
  21.3 4.0 copy-start
  21.4 4.0 copy-start.3
Sparse Core Ops, SparseCore 0:
  10.1 69.3 all-gather.4
  357.7 78.4 all-gather.6
where the time goes:
time: 450 us; the launch traced here: 449 us
  blocking collectives  206 us (46%)
  other arithmetic  60.1 us (13%)
  waiting for transfers between devices  56.8 us (13%)
  matrix products  42.2 us (9%)
  local copies, waits for them, and re-layouts  34.8 us (8%)
  loops' own time  32.5 us (7%)
  between operations  16.1 us (4%)
    all_to_all x1, blocking collectives, summed_on_arrival(): lax.all_to_all(tiles, axis, split_axis=0, concat_axis=0, tiled=True)  135 us
    psum x4, blocking collectives, over_axes(): return functools.reduce(lax.psum, axes, shard)  71.9 us
    all_gather x1, waiting for transfers between devices, shards(): piece = lax.all_gather(references, 'gx', axis=0, tiled=True)  53.3 us
    another operation x1, loops' own time, shards(): lax.map(lambda offset: class_terms(offset), jnp.arange(references.shape[0...  31.4 us
    convert_element_type x16, other arithmetic, add_class(): lax.dynamic_index_in_dim(piece, offset, 0, keepdims=False)  14.8 us
    dot_general x16, matrix products, add_class(): jnp.dot(power_table, amplitude.T, precision=lax.Precision.HIGHEST, prefer...  14.7 us
    dynamic_update_slice x16, other arithmetic, shards(): lax.map(lambda offset: class_terms(offset), jnp.arange(references.shape[0...  11.7 us
    cos x32, other arithmetic, phase_tables(): return (jnp.cos(angles), jnp.sin(angles))  11 us
  transfers between devices with their start and end apart: 2, of which 2 were waited for; matrix products, arithmetic and copies ran while one was open for 5% of the time, Pallas kernels for 0%

commit v1 on v0

v1 whole, which is shorter than its diff:
```python
import functools

import jax
import jax.numpy as jnp
import ml_dtypes
import numpy as np
from jax import lax
from jax.experimental import pallas as pl
from jax.experimental.pallas import tpu as pltpu
from jax.sharding import PartitionSpec as P

L = 64
R = 12
NS = 8
G = 128
HALF = 2048
FR = 4096
PD = 64
NZ = 16
NC = 16
KR = R * NZ
BF = jnp.bfloat16
F32 = jnp.float32
MESH = pl.DeviceIdType.MESH


def dft_tables():
    y2, x = np.divmod(np.arange(512), 64)
    low, v = np.divmod(np.arange(256), 32)
    turns = (8 * y2[:, None] * low[None] + x[:, None] * v[None]) % 64
    angle = turns * (2.0 * np.pi / 64)
    table = np.concatenate([np.cos(angle), -np.sin(angle)], axis=1) / 64
    high = table.astype(ml_dtypes.bfloat16)
    rest = (table - high.astype(np.float64)).astype(ml_dtypes.bfloat16)
    twist = (np.arange(8)[:, None] * low[None]) * (2.0 * np.pi / 64)
    twiddle = np.stack([np.cos(twist), -np.sin(twist)]).astype(np.float32)
    return np.stack([high, rest]), twiddle


def c_add(a, b):
    return a[0] + b[0], a[1] + b[1]


def c_sub(a, b):
    return a[0] - b[0], a[1] - b[1]


def c_mul(a, b):
    return a[0] * b[0] - a[1] * b[1], a[0] * b[1] + a[1] * b[0]


def minus_i(a):
    return a[1], -a[0]


def dft8(a):
    root = np.float32(np.sqrt(0.5))
    s = [c_add(a[n], a[n + 4]) for n in range(4)]
    d = [c_sub(a[n], a[n + 4]) for n in range(4)]
    even, odd = c_add(s[0], s[2]), c_add(s[1], s[3])
    x0, x4 = c_add(even, odd), c_sub(even, odd)
    even, odd = c_sub(s[0], s[2]), minus_i(c_sub(s[1], s[3]))
    x2, x6 = c_add(even, odd), c_sub(even, odd)
    w1 = [(root * (q[0] + q[1]), root * (q[1] - q[0])) for q in (d[1], d[3])]
    w3 = [(root * (q[1] - q[0]), -root * (q[0] + q[1])) for q in (d[1], d[3])]
    even, odd = c_add(d[0], minus_i(d[2])), c_add(w1[0], w3[1])
    x1, x5 = c_add(even, odd), c_sub(even, odd)
    even, odd = c_sub(d[0], minus_i(d[2])), c_add(w3[0], w1[1])
    x3, x7 = c_add(even, odd), c_sub(even, odd)
    return [x0, x1, x2, x3, x4, x5, x6, x7]


def two_parts(value):
    high = value.astype(BF)
    return high, (value - high.astype(F32)).astype(BF)


def dot_nt(a, b):
    return lax.dot_general(a, b, (((1,), (1,)), ((), ())), preferred_element_type=F32)


def dot_nn(a, b):
    return jnp.dot(a, b, preferred_element_type=F32)


def sine_of(turns):
    t = jnp.bitwise_and(turns, 63)
    half = jnp.bitwise_and(t, 31)
    quarter = jnp.minimum(half, 32 - half)
    a = quarter.astype(F32) * np.float32(np.pi / 32)
    q = a * a
    poly = np.float32(-2.5052108385441720e-08)
    for c in (2.7557319223985893e-06, -1.9841269841269841e-04, 8.3333333333333332e-03, -1.6666666666666666e-01):
        poly = poly * q + np.float32(c)
    value = a + a * (q * poly)
    return jnp.where(t >= 32, -value, value)


def kernel(
    part_hbm, refs, slot_class, log_prior, shifts, ids, ctf_hbm, noise, dft_hbm, twiddle,
    out, ctf_out, ev_out,
    pv, ctf, dft, pd, tt, cosb, sinb, wh, pw, vv, dps, a_all, amph, ampl, acc, wt,
    send_a, a16, recv_a, a32, sbuf, own_s, send_x, recv_x, send_s, recv_s,
    ssum, stage, send_3, recv_3, fin, ctf2,
    load_sem, s_a1, r_a1, s_a2, r_a2, s_a3, r_a3, s_x, r_x, s_s, r_s, s_3, r_3, s_4, r_4, s_5, r_5,
):
    z = lax.axis_index("gx")
    g = lax.axis_index("gy")
    chip, core = g // 2, g % 2
    cx, cy = chip // 4, chip % 4
    mate = 2 * chip + 1 - core

    def ahead(d):
        return ((cx + d // 4) % 4) * 4 + (cy + d % 4) % 4

    def behind(d):
        return ((cx + 4 - d // 4) % 4) * 4 + (cy + 4 - d % 4) % 4

    def send(src, dst, s, r, to):
        pltpu.make_async_remote_copy(
            src_ref=src, dst_ref=dst, send_sem=s, recv_sem=r, device_id=to, device_id_type=MESH
        ).start()

    def wait(ref, sem):
        pltpu.make_async_copy(ref, ref, sem).wait()

    def loop(lo, hi, body):
        def step(i, carry):
            body(i)
            return carry

        lax.fori_loop(lo, hi, step, 0)

    def lanes(index, width=128):
        return pl.ds(pl.multiple_of(index * width, width), width)

    loads = [
        pltpu.make_async_copy(ctf_hbm, ctf, load_sem.at[0]),
        pltpu.make_async_copy(part_hbm, pv, load_sem.at[1]),
        pltpu.make_async_copy(dft_hbm, dft, load_sem.at[2]),
    ]
    for load in loads:
        load.start()

    barrier = pltpu.get_barrier_semaphore()

    def greet(d):
        pl.semaphore_signal(barrier, inc=1, device_id=((z + d) % NZ, g), device_id_type=MESH)
        pl.semaphore_signal(barrier, inc=1, device_id=(z, 2 * ahead(d) + core), device_id_type=MESH)

    loop(1, 16, greet)
    pl.semaphore_signal(barrier, inc=1, device_id=(z, mate), device_id_type=MESH)

    a16[...] = jnp.zeros((16, 128), F32)
    a16[0:R, :] = refs[0, :, lanes(core * 16 + chip)].astype(F32)
    send_a[...] = a16[...].astype(BF)
    pl.semaphore_wait(barrier, 31)

    def start_a1(d):
        to = (z + d) % NZ
        send(send_a, recv_a.at[z], s_a1, r_a1, (to, g))

    loop(1, 16, start_a1)
    recv_a[pl.ds(z, 1)] = send_a[...][None]

    freq = lax.broadcasted_iota(jnp.int32, (NS, HALF), 1)
    turns = (freq // 32) * shifts[:, 0:1] + (freq % 32) * shifts[:, 1:2]
    cosb[...] = sine_of(turns + 16)
    sinb[...] = sine_of(turns)
    inv_noise = 1.0 / noise[...]
    hot_t = (lax.broadcasted_iota(jnp.int32, (G, PD), 0) == ids[...]).astype(F32)
    hot = hot_t.T.astype(BF)
    loads[0].wait()
    table_high, table_low = two_parts(ctf[...])
    rows = dot_nn(hot, table_high) + dot_nn(hot, table_low)
    wh[...] = rows * inv_noise
    power_high, power_low = two_parts(rows * rows * inv_noise)
    pw[0:PD, :] = power_high
    pw[PD : 2 * PD, :] = power_low
    square_high, square_low = two_parts(ctf[...] * ctf[...])
    ctf2[0:G, :] = square_high
    ctf2[G : 2 * G, :] = square_low

    wait(recv_a.at[pl.ds(0, 15)], r_a1)
    for k in range(NZ):
        a32[pl.ds(k, R, stride=NZ), :] = recv_a[k].astype(F32)[0:R]
    a_all[:, lanes(g)] = a32[...].astype(BF)
    mine = a_all.at[:, lanes(g)]

    def start_a2(d):
        send(mine, mine, s_a2, r_a2.at[d], (z, 2 * ahead(d) + core))

    loop(1, 16, start_a2)
    send(mine, mine, s_a3, r_a3, (z, mate))

    lane = lax.broadcasted_iota(jnp.int32, (PD, 128), 1)
    loads[1].wait()
    for q in range(4):
        for r in range(4):
            a = pv[:, (q + 8 * r) * 128 : (q + 8 * r + 1) * 128].astype(F32)
            b = pv[:, (q + 8 * r + 4) * 128 : (q + 8 * r + 5) * 128].astype(F32)
            first = jnp.where(lane < 64, a, pltpu.roll(b, 64, 1))
            second = jnp.where(lane < 64, pltpu.roll(a, 64, 1), b)
            cols = slice(r * 128, (r + 1) * 128)
            pd[2 * q * PD : (2 * q + 1) * PD, cols] = first.astype(BF)
            pd[(2 * q + 1) * PD : (2 * q + 2) * PD, cols] = second.astype(BF)
    loads[2].wait()
    tt[...] = dot_nn(pd[...], dft[0]) + dot_nn(pd[...], dft[1])

    def spectrum(pb):
        at = pl.multiple_of(pb * 16, 16)
        power = jnp.zeros((16, 128), F32)
        for h in range(2):
            cols = slice(h * 128, (h + 1) * 128)
            terms = []
            for y1 in range(8):
                where = pl.ds(pl.multiple_of(y1 * PD + at, 16), 16)
                t = tt[where, h * 128 : h * 128 + 128], tt[where, 256 + h * 128 : 256 + h * 128 + 128]
                if y1:
                    t = c_mul(t, (twiddle[0, y1 : y1 + 1, cols], twiddle[1, y1 : y1 + 1, cols]))
                terms.append(t)
            for m, (re, im) in enumerate(dft8(terms)):
                block = 2 * m + h
                f = slice(block * 128, block * 128 + 128)
                power = power + (re * re + im * im) * (1.0 / noise[:, f])
                factor = wh[pl.ds(at, 16), f]
                re, im = re * factor, im * factor
                for s in range(NS):
                    c, n = cosb[s : s + 1, f], sinb[s : s + 1, f]
                    where = pl.ds(pl.multiple_of(s * PD + at, 16), 16)
                    vv[where, block * 256 : block * 256 + 128] = (re * c - im * n).astype(BF)
                    vv[where, block * 256 + 128 : block * 256 + 256] = (re * n + im * c).astype(BF)
        dps[pl.ds(at, 16), :] = power

    loop(0, 4, spectrum)

    slot = lax.broadcasted_iota(jnp.int32, (1, KR), 1) % NZ
    prior = jnp.zeros((1, KR), F32)
    for k in range(NZ):
        prior = jnp.where(slot == k, log_prior[slot_class[k]], prior)

    def forward(d):
        block = a_all.at[:, lanes(2 * behind(d) + core)]
        wait(block, r_a2.at[d])
        send(block, block, s_a3, r_a3, (z, mate))

    loop(1, 16, forward)
    wait(a_all.at[:, pl.ds(0, HALF)], r_a3)

    def amplitude(b):
        both = a_all[:, lanes(b, 256)].astype(F32)
        re, im = both[:, :128], both[:, 128:]
        high, low = two_parts(re * re + im * im)
        amph[:, lanes(b)] = high
        ampl[:, lanes(b)] = low

    loop(0, 16, amplitude)
    both = dot_nt(pw[...], amph[...])
    own_power = both[0:PD] + both[PD : 2 * PD] + dot_nt(pw[0:PD, :], ampl[...])
    base = prior - 0.5 * own_power
    acc[...] = dot_nt(vv[...], a_all[...])

    top = jnp.full((PD, KR), -jnp.inf, F32)
    for s in range(NS):
        value = acc[s * PD : (s + 1) * PD, :] + base
        acc[s * PD : (s + 1) * PD, :] = value
        top = jnp.maximum(top, value)
    top = jnp.max(top, axis=1, keepdims=True)
    total = jnp.zeros((PD, KR), F32)
    for s in range(NS):
        value = jnp.exp(acc[s * PD : (s + 1) * PD, :] - top)
        acc[s * PD : (s + 1) * PD, :] = value
        total = total + value
    total = jnp.sum(total, axis=1, keepdims=True)
    scale = 1.0 / total
    data_power = jnp.sum(dps[...], axis=1, keepdims=True)
    evidence = top + jnp.log(total) - 0.5 * data_power
    evidence = jnp.sum(evidence, axis=0, keepdims=True)
    scale2 = jnp.concatenate([scale, scale], axis=0)
    for s in range(NS // 2):
        w = acc[s * 128 : (s + 1) * 128, :] * scale2
        wt[:, s * 128 : (s + 1) * 128] = w.T.astype(BF)

    hot8 = jnp.concatenate([hot] * NS, axis=0)
    by_group = dot_nn(wt[...], hot8)
    groups = by_group[0:NZ]
    for r in range(1, R):
        groups = groups + by_group[r * NZ : (r + 1) * NZ]

    def block_at(i):
        return ahead((i + 1) % 16)

    def moment(i):
        b = block_at(i)
        part = dot_nn(wt[...], vv[:, lanes(b, 256)])
        sbuf[0] = part[:, :128]
        sbuf[1] = part[:, 128:]
        own_s[b] = sbuf[core]
        send_x[b] = sbuf[1 - core].astype(BF)
        send(send_x.at[b], recv_x.at[b], s_x, r_x.at[b], (z, mate))

    def pair_sum(i):
        b = block_at(i)
        wait(recv_x.at[b], r_x.at[b])
        return (own_s[b] + recv_x[b].astype(F32)).astype(BF), b

    def plane(i):
        value, b = pair_sum(i)
        send_s[b] = value
        send(send_s.at[b], recv_s.at[chip], s_s, r_s, (z, 2 * b + core))

    LAG = 3
    loop(0, LAG, moment)

    def both_steps(i):
        moment(i)
        plane(i - LAG)

    loop(LAG, 16, both_steps)
    loop(16 - LAG, 15, plane)
    value, _ = pair_sum(15)
    recv_s[pl.ds(chip, 1)] = value[None]

    gw_high, gw_low = two_parts(groups)
    ev_high, ev_low = two_parts(evidence)
    for k in range(NZ):
        stage[k, R : R + 1, :] = gw_high[k : k + 1].astype(F32)
        stage[k, R + 1 : R + 2, :] = gw_low[k : k + 1].astype(F32)
        stage[k, R + 2 : R + 3, :] = jnp.broadcast_to(ev_high.astype(F32), (1, 128))
        stage[k, R + 3 : R + 4, :] = jnp.broadcast_to(ev_low.astype(F32), (1, 128))

    wait(recv_s.at[pl.ds(0, 15)], r_s)
    total_s = recv_s[0].astype(F32)
    for t in range(1, NC):
        total_s = total_s + recv_s[t].astype(F32)
    ssum[...] = total_s
    for k in range(NZ):
        stage[k, 0:R, :] = ssum[pl.ds(k, R, stride=NZ), :]
    send_3[...] = stage[...].astype(BF)

    def start_3(d):
        to = (z + d) % NZ
        send(send_3.at[to], recv_3.at[z], s_3, r_3, (to, g))

    loop(1, 16, start_3)
    recv_3[pl.ds(z, 1)] = send_3[pl.ds(z, 1)]
    wait(recv_3.at[pl.ds(0, 15)], r_3)
    last = recv_3[0].astype(F32)
    for t in range(1, NZ):
        last = last + recv_3[t].astype(F32)
    fin[chip, core] = last
    tile = fin.at[chip, core]
    send(tile, tile, s_4, r_4, (z, mate))
    wait(tile, r_4)
    pair = fin.at[chip]

    def start_5(d):
        send(pair, pair, s_5, r_5, (z, 2 * ahead(d) + core))

    loop(1, 16, start_5)
    wait(fin.at[pl.ds(0, 15)], r_5)

    rest = jnp.zeros((R - 8, 128), F32)
    for t in range(NC):
        for c in range(2):
            at = c * HALF + t * 128
            out[0, :, at : at + 128] = fin[t, c, 0:R, :]
            rest = rest + fin[t, c, R:16, :]
    gw_high, gw_low = two_parts(rest[0:1] + rest[1:2])
    left = jnp.concatenate([gw_high, gw_high], axis=1), jnp.concatenate([gw_low, gw_low], axis=1)
    ctf_out[...] = dot_nn(left[0], ctf2[...]) + dot_nn(left[1], ctf2[...])
    ev_out[...] = (rest[2:3] + rest[3:4]) * (1.0 / (PD * NZ * NC * 2 * HALF))

    wait(recv_a.at[pl.ds(0, 15)], s_a1)
    wait(a_all.at[:, pl.ds(0, 15 * 128)], s_a2)
    wait(a_all.at[:, pl.ds(0, HALF)], s_a3)
    wait(send_x, s_x)
    wait(send_s.at[pl.ds(0, 15)], s_s)
    wait(send_3.at[pl.ds(0, 15)], s_3)
    wait(tile, s_4)
    wait(fin.at[pl.ds(0, 15)], s_5)


def shards(dft, twiddle, particles, references, slot_class, log_prior, shift_offsets, group_ids, ctf_table, noise_power):
    vmem = pl.BlockSpec(memory_space=pltpu.VMEM)
    smem = pl.BlockSpec(memory_space=pltpu.SMEM)
    hbm = pl.BlockSpec(memory_space=pl.ANY)
    dma = pltpu.SemaphoreType.DMA
    class_sums, ctf_power, evidence = pl.pallas_call(
        kernel,
        out_shape=(
            jax.ShapeDtypeStruct((1, R, FR), F32),
            jax.ShapeDtypeStruct((1, HALF), F32),
            jax.ShapeDtypeStruct((1, 128), F32),
        ),
        in_specs=[hbm, vmem, smem, smem, vmem, vmem, hbm, vmem, hbm, vmem],
        out_specs=(vmem, vmem, vmem),
        scratch_shapes=[
            pltpu.VMEM((PD, FR), BF),
            pltpu.VMEM((G, HALF), F32),
            pltpu.VMEM((2, 512, 512), BF),
            pltpu.VMEM((512, 512), BF),
            pltpu.VMEM((512, 512), F32),
            pltpu.VMEM((NS, HALF), F32),
            pltpu.VMEM((NS, HALF), F32),
            pltpu.VMEM((PD, HALF), F32),
            pltpu.VMEM((2 * PD, HALF), BF),
            pltpu.VMEM((NS * PD, FR), BF),
            pltpu.VMEM((PD, 128), F32),
            pltpu.VMEM((KR, FR), BF),
            pltpu.VMEM((KR, HALF), BF),
            pltpu.VMEM((KR, HALF), BF),
            pltpu.VMEM((NS * PD, KR), F32),
            pltpu.VMEM((KR, NS * PD), BF),
            pltpu.VMEM((16, 128), BF),
            pltpu.VMEM((16, 128), F32),
            pltpu.VMEM((NZ, 16, 128), BF),
            pltpu.VMEM((KR, 128), F32),
            pltpu.VMEM((2, KR, 128), F32),
            pltpu.VMEM((NC, KR, 128), F32),
            pltpu.VMEM((NC, KR, 128), BF),
            pltpu.VMEM((NC, KR, 128), BF),
            pltpu.VMEM((NC, KR, 128), BF),
            pltpu.VMEM((NC, KR, 128), BF),
            pltpu.VMEM((KR, 128), F32),
            pltpu.VMEM((NZ, 16, 128), F32),
            pltpu.VMEM((NZ, 16, 128), BF),
            pltpu.VMEM((NZ, 16, 128), BF),
            pltpu.VMEM((NC, 2, 16, 128), F32),
            pltpu.VMEM((2 * G, HALF), BF),
            dma((3,)),
            dma, dma,
            dma, dma((16,)),
            dma, dma,
            dma, dma((16,)),
            dma, dma,
            dma, dma,
            dma, dma,
            dma, dma,
        ],
        compiler_params=pltpu.CompilerParams(
            collective_id=0, has_side_effects=True, vmem_limit_bytes=56 * 1024 * 1024
        ),
    )(
        particles, references, slot_class, log_prior, shift_offsets,
        group_ids.reshape(1, PD), ctf_table, noise_power.reshape(1, HALF), dft, twiddle,
    )
    return class_sums, ctf_power, evidence[0, 0]


def solution(mesh):
    dft, twiddle = dft_tables()
    split = ("gx", "gy")
    in_specs = (P(split, None), P("gx", None, None), P(), P(), P(), P(split), P(), P())
    out_specs = (P("gx", None, None), P("gx", None), P())

    def run(*args):
        body = functools.partial(shards, jnp.asarray(dft), jnp.asarray(twiddle))
        return jax.shard_map(body, mesh=mesh, in_specs=in_specs, out_specs=out_specs, check_vma=False)(*args)

    return run
```

time: 450 us -> 82.9 us (0.18)
  blocking collectives: 206 us -> 0 us
  Pallas kernels: 0 us -> 77.1 us
  other arithmetic: 60.1 us -> 0 us
  waiting for transfers between devices: 56.8 us -> 0 us
  matrix products: 42.2 us -> 0 us
  loops' own time: 32.5 us -> 0 us
  local copies, waits for them, and re-layouts: 34.8 us -> 3.78 us
  between operations: 16.1 us -> 1.82 us
    all_to_all x1 -> x0, blocking collectives: 135 us -> none  [summed_on_arrival(): lax.all_to_all(tiles, axis, split_axis=0, concat_axis=0, tiled=True)]
    pallas_call x0 -> x1, Pallas kernels: none -> 77.1 us  [shards(): pl.pallas_call(kernel, out_shape=(jax.ShapeDtypeStruct((1, R, FR), F32),...]
    psum x4 -> x0, blocking collectives: 71.9 us -> none  [over_axes(): return functools.reduce(lax.psum, axes, shard)]
    all_gather x2 -> x0, waiting for transfers between devices: 56.1 us -> none  [the longest x1 53.3 us: shards(): piece = lax.all_gather(references, 'gx', axis=0, tiled=True)]
    dot_general x70 -> x0, matrix products: 42.2 us -> none  [the longest x16 14.7 us: add_class(): jnp.dot(power_table, amplitude.T, precision=lax.Precision.HIGHEST, prefer...]
    another operation x2 -> x0, loops' own time: 32.5 us -> none  [the longest x1 31.4 us: shards(): lax.map(lambda offset: class_terms(offset), jnp.arange(references.shape[0...]
    reduce_sum x23 -> x0, other arithmetic: 19 us -> none  [the longest x16 8.85 us: class_terms(): jnp.sum(moment_real * cosines[None] - moment_imag * sine_table[None], axi...]
    convert_element_type x16 -> x0, other arithmetic: 14.8 us -> none  [add_class(): lax.dynamic_index_in_dim(piece, offset, 0, keepdims=False)]
  transfers between devices with their start and end apart: 2 -> 0, of which waited for: 2 -> 0; matrix products, arithmetic and copies ran while one was open for 5% -> 0% of each run, Pallas kernels for 0% -> 0%
where the time goes in v1:
time: 82.9 us; the launch traced here: 82.7 us
  Pallas kernels  77.1 us (93%)
  local copies, waits for them, and re-layouts  3.78 us (5%)
  between operations  1.82 us (2%)
    pallas_call x1, Pallas kernels, shards(): pl.pallas_call(kernel, out_shape=(jax.ShapeDtypeStruct((1, R, FR), F32),...  77.1 us
    unnamed x9, local copies, waits for them, and re-layouts  3.78 us

profile of v1, /device:TPU:1, one launch (start us, length us, event | category | flops | bytes accessed | tf_op | source)
XLA Modules:
  0.0 82.7 jit_solution(4520743008966281214)
XLA Ops:
  0.6 0.0 copy-start.1
  0.6 0.7 copy-done.1
  1.3 0.7 copy.13.shifts
  2.0 77.1 %shard_map.121 = (f32[1,12,4096]{2,1,0:T(8,128)}, f32[1,2048]{1,0:T(1,128)}, f32[1,128]{1,0:T(1,128)}) custom-call(bf16[64,4096]{1,0:T(8,128)(2,1)} %part_hbm.1, bf16[1,12,4096]{2,1,0:T(8,128)(2,1)} %refs.1, s32[16]{0:T(128)} %slot_class.1, f32[16]{0:T(128)} %log_prior.1, s32[8,2]{1,0:T(8,128)} %copy.13.shifts, s32[1,64]{1,0:T(1,128)} %bitcast.5, ...), custom_call_target="tpu_custom_call" | custom-call | tf_op jit(solution)/shard_map/pallas_call | solution.py:389
  79.0 0.0 copy-start
  79.1 1.8 %copy.14 = f32[1,12,4096]{2,0,1:T(1,128)} copy(f32[1,12,4096]{2,1,0:T(8,128)} %get-tuple-element.9) | data formatting | bytes 393216
  80.9 0.0 copy-done
  80.9 0.0 copy-start.2
  80.9 0.6 copy.17
  81.5 0.0 copy-done.2
Async XLA Ops:
  0.6 0.7 copy-start.1
  79.0 1.8 %copy-start = (f32[1,2048]{1,0:T(1,128)S(1)}, f32[1,2048]{1,0:T(1,128)}, u32[]{:S(2)}) copy-start(f32[1,2048]{1,0:T(1,128)} %get-tuple-element.16) | copy-start | bytes 24580
  80.9 0.6 copy-start.2

commit v2 on v1

--- a/solution.py
+++ b/solution.py
@@ -18,6 +18,8 @@
 PD = 64
 NZ = 16
 NC = 16
+HAND_LAG = 3
+LAG = 4
 KR = R * NZ
 BF = jnp.bfloat16
 F32 = jnp.float32
@@ -99,10 +101,10 @@
 def kernel(
     part_hbm, refs, slot_class, log_prior, shifts, ids, ctf_hbm, noise, dft_hbm, twiddle,
     out, ctf_out, ev_out,
-    pv, ctf, dft, pd, tt, cosb, sinb, wh, pw, vv, dps, a_all, amph, ampl, acc, wt,
+    pv, ctf, dft, pd, tt, cosb, sinb, wh, pw, vv, dps, a_all, power, acc, wt,
     send_a, a16, recv_a, a32, sbuf, own_s, send_x, recv_x, send_s, recv_s,
     ssum, stage, send_3, recv_3, fin, ctf2,
-    load_sem, s_a1, r_a1, s_a2, r_a2, s_a3, r_a3, s_x, r_x, s_s, r_s, s_3, r_3, s_4, r_4, s_5, r_5,
+    load_sem, s_a1, r_a1, s_a2, r_a2, s_a3, r_a3, s_x, r_x, s_s, r_s, s_3, r_3, s_5, r_5,
 ):
     z = lax.axis_index("gx")
     g = lax.axis_index("gy")
@@ -146,7 +148,8 @@
 
     def greet(d):
         pl.semaphore_signal(barrier, inc=1, device_id=((z + d) % NZ, g), device_id_type=MESH)
-        pl.semaphore_signal(barrier, inc=1, device_id=(z, 2 * ahead(d) + core), device_id_type=MESH)
+        pl.semaphore_signal(barrier, inc=1, device_id=(z, 2 * ahead(d)), device_id_type=MESH)
+        pl.semaphore_signal(barrier, inc=1, device_id=(z, 2 * ahead(d) + 1), device_id_type=MESH)
 
     loop(1, 16, greet)
     pl.semaphore_signal(barrier, inc=1, device_id=(z, mate), device_id_type=MESH)
@@ -154,7 +157,7 @@
     a16[...] = jnp.zeros((16, 128), F32)
     a16[0:R, :] = refs[0, :, lanes(core * 16 + chip)].astype(F32)
     send_a[...] = a16[...].astype(BF)
-    pl.semaphore_wait(barrier, 31)
+    pl.semaphore_wait(barrier, 46)
 
     def start_a1(d):
         to = (z + d) % NZ
@@ -164,7 +167,12 @@
     recv_a[pl.ds(z, 1)] = send_a[...][None]
 
     freq = lax.broadcasted_iota(jnp.int32, (NS, HALF), 1)
-    turns = (freq // 32) * shifts[:, 0:1] + (freq % 32) * shifts[:, 1:2]
+    which = lax.broadcasted_iota(jnp.int32, (NS, 128), 0)
+    down, along = jnp.zeros((NS, 128), jnp.int32), jnp.zeros((NS, 128), jnp.int32)
+    for s in range(NS):
+        down = jnp.where(which == s, shifts[0, s], down)
+        along = jnp.where(which == s, shifts[1, s], along)
+    turns = (freq // 32) * down[:, 0:1] + (freq % 32) * along[:, 0:1]
     cosb[...] = sine_of(turns + 16)
     sinb[...] = sine_of(turns)
     inv_noise = 1.0 / noise[...]
@@ -191,7 +199,7 @@
         send(mine, mine, s_a2, r_a2.at[d], (z, 2 * ahead(d) + core))
 
     loop(1, 16, start_a2)
-    send(mine, mine, s_a3, r_a3, (z, mate))
+    send(mine, mine, s_a3, r_a3.at[0], (z, mate))
 
     lane = lax.broadcasted_iota(jnp.int32, (PD, 128), 1)
     loads[1].wait()
@@ -209,7 +217,7 @@
 
     def spectrum(pb):
         at = pl.multiple_of(pb * 16, 16)
-        power = jnp.zeros((16, 128), F32)
+        total = jnp.zeros((16, 128), F32)
         for h in range(2):
             cols = slice(h * 128, (h + 1) * 128)
             terms = []
@@ -222,7 +230,7 @@
             for m, (re, im) in enumerate(dft8(terms)):
                 block = 2 * m + h
                 f = slice(block * 128, block * 128 + 128)
-                power = power + (re * re + im * im) * (1.0 / noise[:, f])
+                total = total + (re * re + im * im) * (1.0 / noise[:, f])
                 factor = wh[pl.ds(at, 16), f]
                 re, im = re * factor, im * factor
                 for s in range(NS):
@@ -230,7 +238,7 @@
                     where = pl.ds(pl.multiple_of(s * PD + at, 16), 16)
                     vv[where, block * 256 : block * 256 + 128] = (re * c - im * n).astype(BF)
                     vv[where, block * 256 + 128 : block * 256 + 256] = (re * n + im * c).astype(BF)
-        dps[pl.ds(at, 16), :] = power
+        dps[pl.ds(at, 16), :] = total
 
     loop(0, 4, spectrum)
 
@@ -239,26 +247,32 @@
     for k in range(NZ):
         prior = jnp.where(slot == k, log_prior[slot_class[k]], prior)
 
+    acc[...] = jnp.zeros((NS * PD, KR), F32)
+    power[...] = jnp.zeros((2 * PD, KR), F32)
+
     def forward(d):
         block = a_all.at[:, lanes(2 * behind(d) + core)]
         wait(block, r_a2.at[d])
-        send(block, block, s_a3, r_a3, (z, mate))
-
-    loop(1, 16, forward)
-    wait(a_all.at[:, pl.ds(0, HALF)], r_a3)
-
-    def amplitude(b):
-        both = a_all[:, lanes(b, 256)].astype(F32)
-        re, im = both[:, :128], both[:, 128:]
+        send(block, block, s_a3, r_a3.at[d], (z, mate))
+
+    def score(d):
+        b = behind(d)
+        wait(a_all.at[:, lanes(2 * b + 1 - core)], r_a3.at[d])
+        both = a_all[:, lanes(b, 256)]
+        acc[...] += dot_nt(vv[:, lanes(b, 256)], both)
+        re, im = both[:, :128].astype(F32), both[:, 128:].astype(F32)
         high, low = two_parts(re * re + im * im)
-        amph[:, lanes(b)] = high
-        ampl[:, lanes(b)] = low
-
-    loop(0, 16, amplitude)
-    both = dot_nt(pw[...], amph[...])
-    own_power = both[0:PD] + both[PD : 2 * PD] + dot_nt(pw[0:PD, :], ampl[...])
-    base = prior - 0.5 * own_power
-    acc[...] = dot_nt(vv[...], a_all[...])
+        power[...] += dot_nt(pw[:, lanes(b)], high)
+        power[0:PD, :] += dot_nt(pw[0:PD, lanes(b)], low)
+
+    def forward_score(d):
+        forward(d)
+        score(d - HAND_LAG)
+
+    loop(1, HAND_LAG, forward)
+    loop(HAND_LAG, 16, forward_score)
+    loop(16 - HAND_LAG, 16, score)
+    base = prior - 0.5 * (power[0:PD, :] + power[PD : 2 * PD, :])
 
     top = jnp.full((PD, KR), -jnp.inf, F32)
     for s in range(NS):
@@ -281,12 +295,6 @@
         w = acc[s * 128 : (s + 1) * 128, :] * scale2
         wt[:, s * 128 : (s + 1) * 128] = w.T.astype(BF)
 
-    hot8 = jnp.concatenate([hot] * NS, axis=0)
-    by_group = dot_nn(wt[...], hot8)
-    groups = by_group[0:NZ]
-    for r in range(1, R):
-        groups = groups + by_group[r * NZ : (r + 1) * NZ]
-
     def block_at(i):
         return ahead((i + 1) % 16)
 
@@ -309,7 +317,6 @@
         send_s[b] = value
         send(send_s.at[b], recv_s.at[chip], s_s, r_s, (z, 2 * b + core))
 
-    LAG = 3
     loop(0, LAG, moment)
 
     def both_steps(i):
@@ -321,6 +328,11 @@
     value, _ = pair_sum(15)
     recv_s[pl.ds(chip, 1)] = value[None]
 
+    hot8 = jnp.concatenate([hot] * NS, axis=0)
+    by_group = dot_nn(wt[...], hot8)
+    groups = by_group[0:NZ]
+    for r in range(1, R):
+        groups = groups + by_group[r * NZ : (r + 1) * NZ]
     gw_high, gw_low = two_parts(groups)
     ev_high, ev_low = two_parts(evidence)
     for k in range(NZ):
@@ -348,24 +360,29 @@
     last = recv_3[0].astype(F32)
     for t in range(1, NZ):
         last = last + recv_3[t].astype(F32)
-    fin[chip, core] = last
-    tile = fin.at[chip, core]
-    send(tile, tile, s_4, r_4, (z, mate))
-    wait(tile, r_4)
-    pair = fin.at[chip]
+    a16[...] = last
+    for row in (R, R + 2):
+        high, low = two_parts(last[row : row + 1] + last[row + 1 : row + 2])
+        a16[row : row + 1, :] = high.astype(F32)
+        a16[row + 1 : row + 2, :] = low.astype(F32)
+    fin[pl.ds(g, 1)] = a16[...].astype(BF)[None]
+    tile = fin.at[g]
 
     def start_5(d):
-        send(pair, pair, s_5, r_5, (z, 2 * ahead(d) + core))
+        for c in range(2):
+            send(tile, tile, s_5, r_5, (z, 2 * ahead(d) + c))
 
     loop(1, 16, start_5)
-    wait(fin.at[pl.ds(0, 15)], r_5)
+    send(tile, tile, s_5, r_5, (z, mate))
+    wait(fin.at[pl.ds(0, 31)], r_5)
 
     rest = jnp.zeros((R - 8, 128), F32)
     for t in range(NC):
         for c in range(2):
             at = c * HALF + t * 128
-            out[0, :, at : at + 128] = fin[t, c, 0:R, :]
-            rest = rest + fin[t, c, R:16, :]
+            block = fin[2 * t + c].astype(F32)
+            out[:, 0, at : at + 128] = block[0:R]
+            rest = rest + block[R:16]
     gw_high, gw_low = two_parts(rest[0:1] + rest[1:2])
     left = jnp.concatenate([gw_high, gw_high], axis=1), jnp.concatenate([gw_low, gw_low], axis=1)
     ctf_out[...] = dot_nn(left[0], ctf2[...]) + dot_nn(left[1], ctf2[...])
@@ -377,8 +394,7 @@
     wait(send_x, s_x)
     wait(send_s.at[pl.ds(0, 15)], s_s)
     wait(send_3.at[pl.ds(0, 15)], s_3)
-    wait(tile, s_4)
-    wait(fin.at[pl.ds(0, 15)], s_5)
+    wait(fin.at[pl.ds(0, 31)], s_5)
 
 
 def shards(dft, twiddle, particles, references, slot_class, log_prior, shift_offsets, group_ids, ctf_table, noise_power):
@@ -389,11 +405,11 @@
     class_sums, ctf_power, evidence = pl.pallas_call(
         kernel,
         out_shape=(
-            jax.ShapeDtypeStruct((1, R, FR), F32),
+            jax.ShapeDtypeStruct((R, 1, FR), F32),
             jax.ShapeDtypeStruct((1, HALF), F32),
             jax.ShapeDtypeStruct((1, 128), F32),
         ),
-        in_specs=[hbm, vmem, smem, smem, vmem, vmem, hbm, vmem, hbm, vmem],
+        in_specs=[hbm, vmem, smem, smem, smem, vmem, hbm, vmem, hbm, vmem],
         out_specs=(vmem, vmem, vmem),
         scratch_shapes=[
             pltpu.VMEM((PD, FR), BF),
@@ -408,8 +424,7 @@
             pltpu.VMEM((NS * PD, FR), BF),
             pltpu.VMEM((PD, 128), F32),
             pltpu.VMEM((KR, FR), BF),
-            pltpu.VMEM((KR, HALF), BF),
-            pltpu.VMEM((KR, HALF), BF),
+            pltpu.VMEM((2 * PD, KR), F32),
             pltpu.VMEM((NS * PD, KR), F32),
             pltpu.VMEM((KR, NS * PD), BF),
             pltpu.VMEM((16, 128), BF),
@@ -426,14 +441,13 @@
             pltpu.VMEM((NZ, 16, 128), F32),
             pltpu.VMEM((NZ, 16, 128), BF),
             pltpu.VMEM((NZ, 16, 128), BF),
-            pltpu.VMEM((NC, 2, 16, 128), F32),
+            pltpu.VMEM((2 * NC, 16, 128), BF),
             pltpu.VMEM((2 * G, HALF), BF),
             dma((3,)),
             dma, dma,
             dma, dma((16,)),
-            dma, dma,
             dma, dma((16,)),
-            dma, dma,
+            dma, dma((16,)),
             dma, dma,
             dma, dma,
             dma, dma,
@@ -442,10 +456,10 @@
             collective_id=0, has_side_effects=True, vmem_limit_bytes=56 * 1024 * 1024
         ),
     )(
-        particles, references, slot_class, log_prior, shift_offsets,
+        particles, references, slot_class, log_prior, shift_offsets.T,
         group_ids.reshape(1, PD), ctf_table, noise_power.reshape(1, HALF), dft, twiddle,
     )
-    return class_sums, ctf_power, evidence[0, 0]
+    return class_sums.transpose(1, 0, 2), ctf_power, evidence[0, 0]
 
 
 def solution(mesh):

time: 82.9 us -> 79.1 us (0.954)
  Pallas kernels: 77.1 us -> 74.8 us
  local copies, waits for them, and re-layouts: 3.78 us -> 2.29 us
    pallas_call x1, Pallas kernels: 77.1 us -> 74.8 us  [shards(): pl.pallas_call(kernel, out_shape=(jax.ShapeDtypeStruct((R, 1, FR), F32),...]
    unnamed x9 -> x6, local copies, waits for them, and re-layouts: 3.78 us -> 2.29 us
where the time goes in v2:
time: 79.1 us; the launch traced here: 78.9 us
  Pallas kernels  74.8 us (95%)
  local copies, waits for them, and re-layouts  2.29 us (3%)
  between operations  1.82 us (2%)
    pallas_call x1, Pallas kernels, shards(): pl.pallas_call(kernel, out_shape=(jax.ShapeDtypeStruct((R, 1, FR), F32),...  74.8 us
    unnamed x6, local copies, waits for them, and re-layouts  2.29 us

profile of v2, /device:TPU:1, one launch (start us, length us, event | category | flops | bytes accessed | tf_op | source)
XLA Modules:
  0.0 78.9 jit_solution(13271593630326967895)
XLA Ops:
  0.6 74.8 %shard_map.121 = (f32[12,1,4096]{2,1,0:T(1,128)}, f32[1,2048]{1,0:T(1,128)}, f32[1,128]{1,0:T(1,128)}) custom-call(bf16[64,4096]{1,0:T(8,128)(2,1)} %part_hbm.1, bf16[1,12,4096]{2,1,0:T(8,128)(2,1)} %refs.1, s32[16]{0:T(128)} %slot_class.1, f32[16]{0:T(128)} %log_prior.1, s32[2,8]{1,0:T(2,128)} %bitcast.8, s32[1,64]{1,0:T(1,128)} %bitcast.9, ...), custom_call_target="tpu_custom_call" | custom-call | tf_op jit(solution)/shard_map/pallas_call | solution.py:405
  75.4 0.0 copy-start
  75.5 1.6 %copy.16 = f32[1,12,4096]{2,0,1:T(1,128)} copy(f32[1,12,4096]{2,0,1:T(1,128)} %bitcast.6) | data formatting | bytes 393216
  77.1 0.0 copy-done
  77.1 0.0 copy-start.1
  77.1 0.6 copy.17
  77.7 0.1 copy-done.1
Async XLA Ops:
  75.4 1.6 %copy-start = (f32[1,2048]{1,0:T(1,128)S(1)}, f32[1,2048]{1,0:T(1,128)}, u32[]{:S(2)}) copy-start(f32[1,2048]{1,0:T(1,128)} %get-tuple-element.13) | copy-start | bytes 24580
  77.1 0.7 copy-start.1

commit v3 on v2

--- a/solution.py
+++ b/solution.py
@@ -18,8 +18,8 @@
 PD = 64
 NZ = 16
 NC = 16
-HAND_LAG = 3
 LAG = 4
+HR = R * NZ // 2
 KR = R * NZ
 BF = jnp.bfloat16
 F32 = jnp.float32
@@ -99,12 +99,12 @@
 
 
 def kernel(
-    part_hbm, refs, slot_class, log_prior, shifts, ids, ctf_hbm, noise, dft_hbm, twiddle,
-    out, ctf_out, ev_out,
-    pv, ctf, dft, pd, tt, cosb, sinb, wh, pw, vv, dps, a_all, power, acc, wt,
-    send_a, a16, recv_a, a32, sbuf, own_s, send_x, recv_x, send_s, recv_s,
-    ssum, stage, send_3, recv_3, fin, ctf2,
-    load_sem, s_a1, r_a1, s_a2, r_a2, s_a3, r_a3, s_x, r_x, s_s, r_s, s_3, r_3, s_5, r_5,
+    part_hbm, refs_hbm, slot_hbm, prior_hbm, shifts_hbm, ids_hbm, ctf_hbm, noise_hbm, dft_hbm, twiddle_hbm,
+    fin_out,
+    refs, slot_class, log_prior, shifts, ids, noise, twiddle, pv, ctf, dft, pd, tt, cosb, sinb, wh, pw, vv, dps, a_all, power, acc, wt,
+    send_a, a16, recv_a, a32, sbuf, own_s, send_x, recv_x, send_s, recv_s, send_b, recv_b,
+    ssum, stage, send_3, recv_3, fin,
+    load_sem, s_a1, r_a1, s_a2, s_a2b, r_a2, r_a2b, s_a3, r_a3, s_x, r_x, s_s, r_s, s_b, r_b, s_3, r_3, s_5, r_5,
 ):
     z = lax.axis_index("gx")
     g = lax.axis_index("gy")
@@ -136,36 +136,35 @@
     def lanes(index, width=128):
         return pl.ds(pl.multiple_of(index * width, width), width)
 
+    barrier = pltpu.get_barrier_semaphore()
+
+    def greet_z(d):
+        pl.semaphore_signal(barrier, inc=1, device_id=((z + d) % NZ, g), device_id_type=MESH)
+
+    def greet_plane(d):
+        pl.semaphore_signal(barrier, inc=1, device_id=(z, 2 * ahead(d)), device_id_type=MESH)
+        pl.semaphore_signal(barrier, inc=1, device_id=(z, 2 * ahead(d) + 1), device_id_type=MESH)
+
+    loop(1, 16, greet_z)
     loads = [
-        pltpu.make_async_copy(ctf_hbm, ctf, load_sem.at[0]),
-        pltpu.make_async_copy(part_hbm, pv, load_sem.at[1]),
-        pltpu.make_async_copy(dft_hbm, dft, load_sem.at[2]),
+        pltpu.make_async_copy(src, dst, load_sem.at[n])
+        for n, (src, dst) in enumerate(
+            (
+                (refs_hbm, refs), (shifts_hbm, shifts), (ids_hbm, ids), (noise_hbm, noise), (ctf_hbm, ctf),
+                (part_hbm, pv), (dft_hbm, dft), (twiddle_hbm, twiddle), (slot_hbm, slot_class), (prior_hbm, log_prior),
+            )
+        )
     ]
     for load in loads:
         load.start()
-
-    barrier = pltpu.get_barrier_semaphore()
-
-    def greet(d):
-        pl.semaphore_signal(barrier, inc=1, device_id=((z + d) % NZ, g), device_id_type=MESH)
-        pl.semaphore_signal(barrier, inc=1, device_id=(z, 2 * ahead(d)), device_id_type=MESH)
-        pl.semaphore_signal(barrier, inc=1, device_id=(z, 2 * ahead(d) + 1), device_id_type=MESH)
-
-    loop(1, 16, greet)
+    loop(1, 16, greet_plane)
     pl.semaphore_signal(barrier, inc=1, device_id=(z, mate), device_id_type=MESH)
+    for load in loads[:4]:
+        load.wait()
 
     a16[...] = jnp.zeros((16, 128), F32)
     a16[0:R, :] = refs[0, :, lanes(core * 16 + chip)].astype(F32)
     send_a[...] = a16[...].astype(BF)
-    pl.semaphore_wait(barrier, 46)
-
-    def start_a1(d):
-        to = (z + d) % NZ
-        send(send_a, recv_a.at[z], s_a1, r_a1, (to, g))
-
-    loop(1, 16, start_a1)
-    recv_a[pl.ds(z, 1)] = send_a[...][None]
-
     freq = lax.broadcasted_iota(jnp.int32, (NS, HALF), 1)
     which = lax.broadcasted_iota(jnp.int32, (NS, 128), 0)
     down, along = jnp.zeros((NS, 128), jnp.int32), jnp.zeros((NS, 128), jnp.int32)
@@ -178,31 +177,25 @@
     inv_noise = 1.0 / noise[...]
     hot_t = (lax.broadcasted_iota(jnp.int32, (G, PD), 0) == ids[...]).astype(F32)
     hot = hot_t.T.astype(BF)
-    loads[0].wait()
+    loads[4].wait()
     table_high, table_low = two_parts(ctf[...])
     rows = dot_nn(hot, table_high) + dot_nn(hot, table_low)
     wh[...] = rows * inv_noise
     power_high, power_low = two_parts(rows * rows * inv_noise)
     pw[0:PD, :] = power_high
     pw[PD : 2 * PD, :] = power_low
-    square_high, square_low = two_parts(ctf[...] * ctf[...])
-    ctf2[0:G, :] = square_high
-    ctf2[G : 2 * G, :] = square_low
-
-    wait(recv_a.at[pl.ds(0, 15)], r_a1)
-    for k in range(NZ):
-        a32[pl.ds(k, R, stride=NZ), :] = recv_a[k].astype(F32)[0:R]
-    a_all[:, lanes(g)] = a32[...].astype(BF)
-    mine = a_all.at[:, lanes(g)]
-
-    def start_a2(d):
-        send(mine, mine, s_a2, r_a2.at[d], (z, 2 * ahead(d) + core))
-
-    loop(1, 16, start_a2)
-    send(mine, mine, s_a3, r_a3.at[0], (z, mate))
+
+    pl.semaphore_wait(barrier, 46)
+
+    def start_a1(d):
+        to = (z + d) % NZ
+        send(send_a, recv_a.at[z], s_a1, r_a1, (to, g))
+
+    loop(1, 16, start_a1)
+    recv_a[pl.ds(z, 1)] = send_a[...][None]
 
     lane = lax.broadcasted_iota(jnp.int32, (PD, 128), 1)
-    loads[1].wait()
+    loads[5].wait()
     for q in range(4):
         for r in range(4):
             a = pv[:, (q + 8 * r) * 128 : (q + 8 * r + 1) * 128].astype(F32)
@@ -212,7 +205,8 @@
             cols = slice(r * 128, (r + 1) * 128)
             pd[2 * q * PD : (2 * q + 1) * PD, cols] = first.astype(BF)
             pd[(2 * q + 1) * PD : (2 * q + 2) * PD, cols] = second.astype(BF)
-    loads[2].wait()
+    loads[6].wait()
+    loads[7].wait()
     tt[...] = dot_nn(pd[...], dft[0]) + dot_nn(pd[...], dft[1])
 
     def spectrum(pb):
@@ -242,18 +236,52 @@
 
     loop(0, 4, spectrum)
 
+    loads[8].wait()
+    loads[9].wait()
     slot = lax.broadcasted_iota(jnp.int32, (1, KR), 1) % NZ
     prior = jnp.zeros((1, KR), F32)
     for k in range(NZ):
         prior = jnp.where(slot == k, log_prior[slot_class[k]], prior)
 
+    wait(recv_a.at[pl.ds(0, 15)], r_a1)
+    for k in range(NZ):
+        a32[pl.ds(k, R, stride=NZ), :] = recv_a[k].astype(F32)[0:R]
+    a_all[:, lanes(g)] = a32[...].astype(BF)
+    mine = a_all.at[:, lanes(g)]
+
+    def start_a2(d):
+        send(mine, mine, s_a2, r_a2.at[4 * d], (z, 2 * ahead(4 * d) + core))
+        send(mine, mine, s_a2, r_a2.at[d], (z, 2 * ahead(d) + core))
+
+    loop(1, 4, start_a2)
+    send(mine, mine, s_a3, r_a3.at[0], (z, mate))
+
     acc[...] = jnp.zeros((NS * PD, KR), F32)
     power[...] = jnp.zeros((2 * PD, KR), F32)
 
-    def forward(d):
-        block = a_all.at[:, lanes(2 * behind(d) + core)]
-        wait(block, r_a2.at[d])
+    def hand_on(block, d):
         send(block, block, s_a3, r_a3.at[d], (z, mate))
+
+    def direct(i):
+        for d, rows, first, step in ((4 * i, slice(0, HR), 4 * i, 1), (i, slice(HR, KR), i, 4)):
+            at = lanes(2 * behind(d) + core)
+            block = a_all.at[:, at]
+            wait(block, r_a2.at[d])
+            part = a_all.at[rows, at]
+            for n in range(1, 4):
+                sem = (r_a2 if step == 1 else r_a2b).at[first + n * step]
+                send(part, part, s_a2b, sem, (z, 2 * ahead(n * step) + core))
+            hand_on(block, d)
+
+    def diagonal(n):
+        return (n // 3 + 1) * 4 + n % 3 + 1
+
+    def relayed(n):
+        d = diagonal(n)
+        at = lanes(2 * behind(d) + core)
+        wait(a_all.at[0:HR, at], r_a2.at[d])
+        wait(a_all.at[HR:KR, at], r_a2b.at[d])
+        hand_on(a_all.at[:, at], d)
 
     def score(d):
         b = behind(d)
@@ -265,13 +293,20 @@
         power[...] += dot_nt(pw[:, lanes(b)], high)
         power[0:PD, :] += dot_nt(pw[0:PD, lanes(b)], low)
 
-    def forward_score(d):
-        forward(d)
-        score(d - HAND_LAG)
-
-    loop(1, HAND_LAG, forward)
-    loop(HAND_LAG, 16, forward_score)
-    loop(16 - HAND_LAG, 16, score)
+    def first_steps(n):
+        relayed(n)
+        score(4 * (n + 1))
+        score(n + 1)
+
+    def next_steps(n):
+        relayed(n)
+        score(diagonal(n - 3))
+
+    loop(1, 4, direct)
+    score(0)
+    loop(0, 3, first_steps)
+    loop(3, 9, next_steps)
+    loop(6, 9, lambda n: score(diagonal(n)))
     base = prior - 0.5 * (power[0:PD, :] + power[PD : 2 * PD, :])
 
     top = jnp.full((PD, KR), -jnp.inf, F32)
@@ -314,8 +349,24 @@
 
     def plane(i):
         value, b = pair_sum(i)
+        d = (i + 1) % 16
         send_s[b] = value
-        send(send_s.at[b], recv_s.at[chip], s_s, r_s, (z, 2 * b + core))
+
+        @pl.when(d // 4 > 0)
+        def _():
+            send(send_s.at[b, 0:HR], recv_s.at[0, cx, b % 4], s_s, r_s.at[0], (z, 2 * ((b // 4) * 4 + cy) + core))
+
+        @pl.when(d // 4 == 0)
+        def _():
+            recv_s[0, cx, b % 4] = value[0:HR]
+
+        @pl.when(d % 4 > 0)
+        def _():
+            send(send_s.at[b, HR:KR], recv_s.at[1, cy, b // 4], s_s, r_s.at[1], (z, 2 * (cx * 4 + b % 4) + core))
+
+        @pl.when(d % 4 == 0)
+        def _():
+            recv_s[1, cy, b // 4] = value[HR:KR]
 
     loop(0, LAG, moment)
 
@@ -324,9 +375,7 @@
         plane(i - LAG)
 
     loop(LAG, 16, both_steps)
-    loop(16 - LAG, 15, plane)
-    value, _ = pair_sum(15)
-    recv_s[pl.ds(chip, 1)] = value[None]
+    loop(16 - LAG, 16, plane)
 
     hot8 = jnp.concatenate([hot] * NS, axis=0)
     by_group = dot_nn(wt[...], hot8)
@@ -341,11 +390,25 @@
         stage[k, R + 2 : R + 3, :] = jnp.broadcast_to(ev_high.astype(F32), (1, 128))
         stage[k, R + 3 : R + 4, :] = jnp.broadcast_to(ev_low.astype(F32), (1, 128))
 
-    wait(recv_s.at[pl.ds(0, 15)], r_s)
-    total_s = recv_s[0].astype(F32)
-    for t in range(1, NC):
-        total_s = total_s + recv_s[t].astype(F32)
-    ssum[...] = total_s
+    for half in range(2):
+        wait(recv_s.at[half, pl.ds(0, 3)], r_s.at[half])
+        here, source, step = (cy, cy, 1) if half == 0 else (cx, cx, 4)
+        for n in range(4):
+            to = (here + n) % 4
+            part = recv_s[half, 0, to].astype(F32)
+            for t in range(1, 4):
+                part = part + recv_s[half, t, to].astype(F32)
+            if n:
+                send_b[half, n] = part.astype(BF)
+                send(send_b.at[half, n], recv_b.at[half, source], s_b, r_b.at[half], (z, 2 * ahead(n * step) + core))
+            else:
+                recv_b[half, source] = part.astype(BF)
+    for half in range(2):
+        wait(recv_b.at[half, pl.ds(0, 3)], r_b.at[half])
+        part = recv_b[half, 0].astype(F32)
+        for t in range(1, 4):
+            part = part + recv_b[half, t].astype(F32)
+        ssum[half * HR : (half + 1) * HR, :] = part
     for k in range(NZ):
         stage[k, 0:R, :] = ssum[pl.ds(k, R, stride=NZ), :]
     send_3[...] = stage[...].astype(BF)
@@ -375,43 +438,50 @@
     loop(1, 16, start_5)
     send(tile, tile, s_5, r_5, (z, mate))
     wait(fin.at[pl.ds(0, 31)], r_5)
-
-    rest = jnp.zeros((R - 8, 128), F32)
+    fin_out[...] = fin[...]
+
+    wait(recv_a.at[pl.ds(0, 15)], s_a1)
+    wait(a_all.at[:, pl.ds(0, 6 * 128)], s_a2)
+    wait(a_all.at[0:HR, pl.ds(0, 18 * 128)], s_a2b)
+    wait(a_all.at[:, pl.ds(0, HALF)], s_a3)
+    wait(send_x, s_x)
+    wait(recv_s.at[:, pl.ds(0, 3)], s_s)
+    wait(send_b.at[:, pl.ds(0, 3)], s_b)
+    wait(send_3.at[pl.ds(0, 15)], s_3)
+    wait(fin.at[pl.ds(0, 31)], s_5)
+
+
+def finish(fin, ctf, out, ctf_out, ev_out):
+    rest = jnp.zeros((16 - R, 128), F32)
     for t in range(NC):
         for c in range(2):
-            at = c * HALF + t * 128
             block = fin[2 * t + c].astype(F32)
-            out[:, 0, at : at + 128] = block[0:R]
+            out[pl.ds(c * NC + t, R, stride=2 * NC), :] = block[0:R]
             rest = rest + block[R:16]
-    gw_high, gw_low = two_parts(rest[0:1] + rest[1:2])
-    left = jnp.concatenate([gw_high, gw_high], axis=1), jnp.concatenate([gw_low, gw_low], axis=1)
-    ctf_out[...] = dot_nn(left[0], ctf2[...]) + dot_nn(left[1], ctf2[...])
+    groups = jnp.broadcast_to(rest[0:1] + rest[1:2], (G, 128)).T
+    for t in range(HALF // 128):
+        f = slice(t * 128, (t + 1) * 128)
+        ctf_out[:, f] = jnp.sum(ctf[:, f] * ctf[:, f] * groups, axis=0, keepdims=True)
     ev_out[...] = (rest[2:3] + rest[3:4]) * (1.0 / (PD * NZ * NC * 2 * HALF))
-
-    wait(recv_a.at[pl.ds(0, 15)], s_a1)
-    wait(a_all.at[:, pl.ds(0, 15 * 128)], s_a2)
-    wait(a_all.at[:, pl.ds(0, HALF)], s_a3)
-    wait(send_x, s_x)
-    wait(send_s.at[pl.ds(0, 15)], s_s)
-    wait(send_3.at[pl.ds(0, 15)], s_3)
-    wait(fin.at[pl.ds(0, 31)], s_5)
 
 
 def shards(dft, twiddle, particles, references, slot_class, log_prior, shift_offsets, group_ids, ctf_table, noise_power):
     vmem = pl.BlockSpec(memory_space=pltpu.VMEM)
-    smem = pl.BlockSpec(memory_space=pltpu.SMEM)
     hbm = pl.BlockSpec(memory_space=pl.ANY)
     dma = pltpu.SemaphoreType.DMA
-    class_sums, ctf_power, evidence = pl.pallas_call(
+    tiles = pl.pallas_call(
         kernel,
-        out_shape=(
-            jax.ShapeDtypeStruct((R, 1, FR), F32),
-            jax.ShapeDtypeStruct((1, HALF), F32),
-            jax.ShapeDtypeStruct((1, 128), F32),
-        ),
-        in_specs=[hbm, vmem, smem, smem, smem, vmem, hbm, vmem, hbm, vmem],
-        out_specs=(vmem, vmem, vmem),
+        out_shape=jax.ShapeDtypeStruct((2 * NC, 16, 128), BF),
+        in_specs=[hbm] * 10,
+        out_specs=vmem,
         scratch_shapes=[
+            pltpu.VMEM((1, R, FR), BF),
+            pltpu.SMEM((NZ,), jnp.int32),
+            pltpu.SMEM((NZ,), F32),
+            pltpu.SMEM((2, NS), jnp.int32),
+            pltpu.VMEM((1, PD), jnp.int32),
+            pltpu.VMEM((1, HALF), F32),
+            pltpu.VMEM((2, 8, 256), F32),
             pltpu.VMEM((PD, FR), BF),
             pltpu.VMEM((G, HALF), F32),
             pltpu.VMEM((2, 512, 512), BF),
@@ -436,19 +506,21 @@
             pltpu.VMEM((NC, KR, 128), BF),
             pltpu.VMEM((NC, KR, 128), BF),
             pltpu.VMEM((NC, KR, 128), BF),
-            pltpu.VMEM((NC, KR, 128), BF),
+            pltpu.VMEM((2, 4, 4, HR, 128), BF),
+            pltpu.VMEM((2, 4, HR, 128), BF),
+            pltpu.VMEM((2, 4, HR, 128), BF),
             pltpu.VMEM((KR, 128), F32),
             pltpu.VMEM((NZ, 16, 128), F32),
             pltpu.VMEM((NZ, 16, 128), BF),
             pltpu.VMEM((NZ, 16, 128), BF),
             pltpu.VMEM((2 * NC, 16, 128), BF),
-            pltpu.VMEM((2 * G, HALF), BF),
-            dma((3,)),
+            dma((10,)),
             dma, dma,
+            dma, dma, dma((16,)), dma((16,)),
             dma, dma((16,)),
             dma, dma((16,)),
-            dma, dma((16,)),
-            dma, dma,
+            dma, dma((2,)),
+            dma, dma((2,)),
             dma, dma,
             dma, dma,
         ],
@@ -459,7 +531,17 @@
         particles, references, slot_class, log_prior, shift_offsets.T,
         group_ids.reshape(1, PD), ctf_table, noise_power.reshape(1, HALF), dft, twiddle,
     )
-    return class_sums.transpose(1, 0, 2), ctf_power, evidence[0, 0]
+    class_sums, ctf_power, evidence = pl.pallas_call(
+        finish,
+        out_shape=(
+            jax.ShapeDtypeStruct((R * FR // 128, 128), F32),
+            jax.ShapeDtypeStruct((1, HALF), F32),
+            jax.ShapeDtypeStruct((1, 128), F32),
+        ),
+        in_specs=[vmem, vmem],
+        out_specs=(vmem, vmem, vmem),
+    )(tiles, ctf_table)
+    return class_sums.reshape(1, R, FR), ctf_power, evidence[0, 0]
 
 
 def solution(mesh):

time: 79.1 us -> 72.4 us (0.915)
  Pallas kernels: 74.8 us -> 71.6 us
  local copies, waits for them, and re-layouts: 2.29 us -> 0 us
  between operations: 1.82 us -> 0.64 us
    pallas_call x1 -> x2, Pallas kernels: 74.8 us -> 71.6 us  [the longest x1 69.4 us: shards(): pl.pallas_call(kernel, out_shape=jax.ShapeDtypeStruct((2 * NC, 16, 128),...]
    unnamed x6 -> x0, local copies, waits for them, and re-layouts: 2.29 us -> none
where the time goes in v3:
time: 72.4 us; the launch traced here: 72.2 us
  Pallas kernels  71.6 us (99%)
    pallas_call x1, Pallas kernels, shards(): pl.pallas_call(kernel, out_shape=jax.ShapeDtypeStruct((2 * NC, 16, 128),...  69.4 us
    pallas_call x1, Pallas kernels, shards(): pl.pallas_call(finish, out_shape=(jax.ShapeDtypeStruct((R * FR // 128, 12...  2.21 us

profile of v3, /device:TPU:1, one launch (start us, length us, event | category | flops | bytes accessed | tf_op | source)
XLA Modules:
  0.0 72.2 jit_solution(450097223804316280)
XLA Ops:
  0.6 69.4 %shard_map.121.fin = bf16[32,16,128]{2,1,0:T(8,128)(2,1)} custom-call(bf16[64,4096]{1,0:T(8,128)(2,1)} %part_hbm.1, bf16[1,12,4096]{2,1,0:T(8,128)(2,1)} %refs_hbm.1, s32[16]{0:T(128)} %slot_hbm.1, f32[16]{0:T(128)} %prior_hbm.1, s32[2,8]{1,0:T(2,128)} %bitcast.7, s32[1,64]{1,0:T(1,128)} %bitcast.8, f32[128,2048]{1,0:T(8,128)} %ctf.1, f32[1,2048]{1,0:T(1,128)} %bitcast.6, ...), custom_call_target="tpu_custom_call" | custom-call | tf_op jit(solution)/shard_map/pallas_call | solution.py:472
  70.0 2.2 %shard_map.122 = (f32[384,128]{1,0:T(8,128)}, f32[1,2048]{1,0:T(1,128)}, f32[1,128]{1,0:T(1,128)}) custom-call(bf16[32,16,128]{2,1,0:T(8,128)(2,1)} %shard_map.121.fin, f32[128,2048]{1,0:T(8,128)} %ctf.1), custom_call_target="tpu_custom_call" | custom-call | tf_op jit(solution)/shard_map/pallas_call | solution.py:534

commit v4 on v3

--- a/solution.py
+++ b/solution.py
@@ -18,7 +18,7 @@
 PD = 64
 NZ = 16
 NC = 16
-LAG = 4
+LAG = 8
 HR = R * NZ // 2
 KR = R * NZ
 BF = jnp.bfloat16
@@ -182,8 +182,9 @@
     rows = dot_nn(hot, table_high) + dot_nn(hot, table_low)
     wh[...] = rows * inv_noise
     power_high, power_low = two_parts(rows * rows * inv_noise)
-    pw[0:PD, :] = power_high
-    pw[PD : 2 * PD, :] = power_low
+    for t in range(NC):
+        f = slice(t * 128, (t + 1) * 128)
+        pw[:, t * 384 : (t + 1) * 384] = jnp.concatenate([power_high[:, f], power_low[:, f], power_high[:, f]], axis=1)
 
     pl.semaphore_wait(barrier, 46)
 
@@ -257,7 +258,7 @@
     send(mine, mine, s_a3, r_a3.at[0], (z, mate))
 
     acc[...] = jnp.zeros((NS * PD, KR), F32)
-    power[...] = jnp.zeros((2 * PD, KR), F32)
+    power[...] = jnp.zeros((PD, KR), F32)
 
     def hand_on(block, d):
         send(block, block, s_a3, r_a3.at[d], (z, mate))
@@ -283,31 +284,36 @@
         wait(a_all.at[HR:KR, at], r_a2b.at[d])
         hand_on(a_all.at[:, at], d)
 
-    def score(d):
-        b = behind(d)
-        wait(a_all.at[:, lanes(2 * b + 1 - core)], r_a3.at[d])
-        both = a_all[:, lanes(b, 256)]
-        acc[...] += dot_nt(vv[:, lanes(b, 256)], both)
-        re, im = both[:, :128].astype(F32), both[:, 128:].astype(F32)
-        high, low = two_parts(re * re + im * im)
-        power[...] += dot_nt(pw[:, lanes(b)], high)
-        power[0:PD, :] += dot_nt(pw[0:PD, lanes(b)], low)
+    def score(*offsets):
+        pairs, sides, values, powers = [], [], [], []
+        for d in offsets:
+            b = behind(d)
+            wait(a_all.at[:, lanes(2 * b + 1 - core)], r_a3.at[d])
+            both = a_all[:, lanes(b, 256)]
+            pairs.append(both)
+            sides.append(vv[:, lanes(b, 256)])
+            re, im = both[:, :128].astype(F32), both[:, 128:].astype(F32)
+            high, low = two_parts(re * re + im * im)
+            values.extend([high, high, low])
+            powers.append(pw[:, lanes(b, 384)])
+        acc[...] += dot_nt(jnp.concatenate(sides, axis=1), jnp.concatenate(pairs, axis=1))
+        power[...] += dot_nt(jnp.concatenate(powers, axis=1), jnp.concatenate(values, axis=1))
 
     def first_steps(n):
         relayed(n)
-        score(4 * (n + 1))
-        score(n + 1)
-
-    def next_steps(n):
-        relayed(n)
-        score(diagonal(n - 3))
+        score(4 * (n + 1), n + 1)
 
     loop(1, 4, direct)
-    score(0)
     loop(0, 3, first_steps)
-    loop(3, 9, next_steps)
-    loop(6, 9, lambda n: score(diagonal(n)))
-    base = prior - 0.5 * (power[0:PD, :] + power[PD : 2 * PD, :])
+    loop(3, 5, relayed)
+    score(0, diagonal(0))
+    for n in range(2):
+        relayed(2 * n + 5)
+        relayed(2 * n + 6)
+        score(diagonal(2 * n + 1), diagonal(2 * n + 2))
+    for n in range(2, 4):
+        score(diagonal(2 * n + 1), diagonal(2 * n + 2))
+    base = prior - 0.5 * power[...]
 
     top = jnp.full((PD, KR), -jnp.inf, F32)
     for s in range(NS):
@@ -331,7 +337,7 @@
         wt[:, s * 128 : (s + 1) * 128] = w.T.astype(BF)
 
     def block_at(i):
-        return ahead((i + 1) % 16)
+        return ahead(5 * (i + 1) % 16)
 
     def moment(i):
         b = block_at(i)
@@ -349,7 +355,7 @@
 
     def plane(i):
         value, b = pair_sum(i)
-        d = (i + 1) % 16
+        d = 5 * (i + 1) % 16
         send_s[b] = value
 
         @pl.when(d // 4 > 0)
@@ -490,11 +496,11 @@
             pltpu.VMEM((NS, HALF), F32),
             pltpu.VMEM((NS, HALF), F32),
             pltpu.VMEM((PD, HALF), F32),
-            pltpu.VMEM((2 * PD, HALF), BF),
+            pltpu.VMEM((PD, NC * 384), BF),
             pltpu.VMEM((NS * PD, FR), BF),
             pltpu.VMEM((PD, 128), F32),
             pltpu.VMEM((KR, FR), BF),
-            pltpu.VMEM((2 * PD, KR), F32),
+            pltpu.VMEM((PD, KR), F32),
             pltpu.VMEM((NS * PD, KR), F32),
             pltpu.VMEM((KR, NS * PD), BF),
             pltpu.VMEM((16, 128), BF),

time: 72.4 us -> 71.1 us (0.982)
  Pallas kernels: 71.6 us -> 70.3 us
    pallas_call x1, Pallas kernels: 69.4 us -> 68.1 us  [shards(): pl.pallas_call(kernel, out_shape=jax.ShapeDtypeStruct((2 * NC, 16, 128),...]
where the time goes in v4:
time: 71.1 us; the launch traced here: 70.9 us
  Pallas kernels  70.3 us (99%)
    pallas_call x1, Pallas kernels, shards(): pl.pallas_call(kernel, out_shape=jax.ShapeDtypeStruct((2 * NC, 16, 128),...  68.1 us
    pallas_call x1, Pallas kernels, shards(): pl.pallas_call(finish, out_shape=(jax.ShapeDtypeStruct((R * FR // 128, 12...  2.21 us

profile of v4, /device:TPU:1, one launch (start us, length us, event | category | flops | bytes accessed | tf_op | source)
XLA Modules:
  0.0 70.9 jit_solution(1501462458054392372)
XLA Ops:
  0.6 68.1 %shard_map.121.fin = bf16[32,16,128]{2,1,0:T(8,128)(2,1)} custom-call(bf16[64,4096]{1,0:T(8,128)(2,1)} %part_hbm.1, bf16[1,12,4096]{2,1,0:T(8,128)(2,1)} %refs_hbm.1, s32[16]{0:T(128)} %slot_hbm.1, f32[16]{0:T(128)} %prior_hbm.1, s32[2,8]{1,0:T(2,128)} %bitcast.7, s32[1,64]{1,0:T(1,128)} %bitcast.8, f32[128,2048]{1,0:T(8,128)} %ctf.1, f32[1,2048]{1,0:T(1,128)} %bitcast.6, ...), custom_call_target="tpu_custom_call" | custom-call | tf_op jit(solution)/shard_map/pallas_call | solution.py:478
  68.7 2.2 %shard_map.122 = (f32[384,128]{1,0:T(8,128)}, f32[1,2048]{1,0:T(1,128)}, f32[1,128]{1,0:T(1,128)}) custom-call(bf16[32,16,128]{2,1,0:T(8,128)(2,1)} %shard_map.121.fin, f32[128,2048]{1,0:T(8,128)} %ctf.1), custom_call_target="tpu_custom_call" | custom-call | tf_op jit(solution)/shard_map/pallas_call | solution.py:540

commit v5 on v4

--- a/solution.py
+++ b/solution.py
@@ -19,6 +19,8 @@
 NZ = 16
 NC = 16
 LAG = 8
+RING_ORDER = (8, 7, 9, 6, 10, 5, 11, 4, 12, 3, 13, 2, 14, 1, 15)
+PLANE_ORDER = (10, 6, 9, 11, 14, 2, 8, 5, 7, 13, 15, 1, 3, 4, 12)
 HR = R * NZ // 2
 KR = R * NZ
 BF = jnp.bfloat16
@@ -192,7 +194,8 @@
         to = (z + d) % NZ
         send(send_a, recv_a.at[z], s_a1, r_a1, (to, g))
 
-    loop(1, 16, start_a1)
+    for d in RING_ORDER:
+        start_a1(d)
     recv_a[pl.ds(z, 1)] = send_a[...][None]
 
     lane = lax.broadcasted_iota(jnp.int32, (PD, 128), 1)
@@ -423,7 +426,8 @@
         to = (z + d) % NZ
         send(send_3.at[to], recv_3.at[z], s_3, r_3, (to, g))
 
-    loop(1, 16, start_3)
+    for d in RING_ORDER:
+        start_3(d)
     recv_3[pl.ds(z, 1)] = send_3[pl.ds(z, 1)]
     wait(recv_3.at[pl.ds(0, 15)], r_3)
     last = recv_3[0].astype(F32)
@@ -441,7 +445,8 @@
         for c in range(2):
             send(tile, tile, s_5, r_5, (z, 2 * ahead(d) + c))
 
-    loop(1, 16, start_5)
+    for d in PLANE_ORDER:
+        start_5(d)
     send(tile, tile, s_5, r_5, (z, mate))
     wait(fin.at[pl.ds(0, 31)], r_5)
     fin_out[...] = fin[...]

time: 71.1 us -> 68.6 us (0.965)
  Pallas kernels: 70.3 us -> 67.7 us
    pallas_call x1, Pallas kernels: 68.1 us -> 65.5 us  [shards(): pl.pallas_call(kernel, out_shape=jax.ShapeDtypeStruct((2 * NC, 16, 128),...]
where the time goes in v5:
time: 68.6 us; the launch traced here: 68.4 us
  Pallas kernels  67.7 us (99%)
    pallas_call x1, Pallas kernels, shards(): pl.pallas_call(kernel, out_shape=jax.ShapeDtypeStruct((2 * NC, 16, 128),...  65.5 us
    pallas_call x1, Pallas kernels, shards(): pl.pallas_call(finish, out_shape=(jax.ShapeDtypeStruct((R * FR // 128, 12...  2.21 us

profile of v5, /device:TPU:1, one launch (start us, length us, event | category | flops | bytes accessed | tf_op | source)
XLA Modules:
  0.0 68.4 jit_solution(6164789934705204700)
XLA Ops:
  0.6 65.5 %shard_map.121.fin = bf16[32,16,128]{2,1,0:T(8,128)(2,1)} custom-call(bf16[64,4096]{1,0:T(8,128)(2,1)} %part_hbm.1, bf16[1,12,4096]{2,1,0:T(8,128)(2,1)} %refs_hbm.1, s32[16]{0:T(128)} %slot_hbm.1, f32[16]{0:T(128)} %prior_hbm.1, s32[2,8]{1,0:T(2,128)} %bitcast.7, s32[1,64]{1,0:T(1,128)} %bitcast.8, f32[128,2048]{1,0:T(8,128)} %ctf.1, f32[1,2048]{1,0:T(1,128)} %bitcast.6, ...), custom_call_target="tpu_custom_call" | custom-call | tf_op jit(solution)/shard_map/pallas_call | solution.py:483
  66.2 2.2 %shard_map.122 = (f32[384,128]{1,0:T(8,128)}, f32[1,2048]{1,0:T(1,128)}, f32[1,128]{1,0:T(1,128)}) custom-call(bf16[32,16,128]{2,1,0:T(8,128)(2,1)} %shard_map.121.fin, f32[128,2048]{1,0:T(8,128)} %ctf.1), custom_call_target="tpu_custom_call" | custom-call | tf_op jit(solution)/shard_map/pallas_call | solution.py:545
